TPU v7x, 256 devices: a whole 4x4x8 slice. The times are simulated.
256 devices in a mesh: img: 32 (over z, x), feat: 8 (over y, core).
Axes of the slice: x: 4, y: 4, z: 8, core: 2. Of those that a mesh axis runs over, the one named last changes fastest.
Arguments:
- view_a: bfloat16 [4096, 2048], P('img'), may hold values from -200 to 200
- view_b: bfloat16 [4096, 2048], P('img'), may hold values from -200 to 200
- projection: bfloat16 [2048, 8192], P(None, 'feat'), may hold values from -2 to 2
Outputs:
- loss: float32 [], replicated
- grad_a: bfloat16 [4096, 2048], P('img', 'feat')
- grad_b: bfloat16 [4096, 2048], P('img', 'feat')
All inputs are finite; a program needn't handle non-finite values.
Results may differ from a plain program's by a relative error of at most 0.018.
Values may be sent and summed in bfloat16 or wider, within the bound.
A program may use at most 128 MiB of HBM per device.

v0:
```python
import jax
import jax.numpy as jnp
from jax import lax
from jax.sharding import PartitionSpec as P

LAMBDA = 0.0051
EPSILON = 1e-05


def gram_rows(local, full):
    return lax.dot_general(
        local, full, (((1,), (1,)), ((), ())), preferred_element_type=jnp.float32
    )


def on_device(view_a, view_b, projection):
    images = view_a.shape[0] * lax.axis_size("img")
    feat_parts = lax.axis_size("feat")
    img_parts = lax.axis_size("img")
    proj_a = jnp.dot(view_a, projection, preferred_element_type=jnp.float32)
    proj_b = jnp.dot(view_b, projection, preferred_element_type=jnp.float32)
    sums = lax.psum(jnp.stack([jnp.sum(proj_a, axis=0), jnp.sum(proj_b, axis=0)]), "img")
    mean_ab = sums / images
    center_a = proj_a - mean_ab[0]
    center_b = proj_b - mean_ab[1]
    squares = lax.psum(
        jnp.stack([jnp.sum(center_a * center_a, axis=0), jnp.sum(center_b * center_b, axis=0)]),
        "img",
    )
    variance = squares / images
    rstd_ab = lax.rsqrt(variance + EPSILON)
    hat_a = center_a * rstd_ab[0]
    hat_b = center_b * rstd_ab[1]
    norm_a = hat_a.astype(jnp.bfloat16)
    norm_b = hat_b.astype(jnp.bfloat16)
    wide_a = norm_a.astype(jnp.float32)
    wide_b = norm_b.astype(jnp.float32)
    corr = lax.psum(jnp.sum(wide_a * wide_b, axis=0), "img") / images
    diag_part = jnp.sum((1.0 - corr) ** 2) - LAMBDA * jnp.sum(corr * corr)
    full_a, full_b = (
        lax.all_gather(norm_a, "img", axis=0, tiled=True),
        lax.all_gather(norm_b, "img", axis=0, tiled=True),
    )
    part_a = gram_rows(norm_a, full_a)
    part_b = gram_rows(norm_b, full_b)
    factor = -2.0 * (1.0 - corr) - 2.0 * LAMBDA * corr
    coef = 2.0 * LAMBDA / images
    gram_a, gram_b = (
        lax.psum(part_a.astype(jnp.bfloat16), "feat").astype(jnp.float32),
        lax.psum(part_b.astype(jnp.bfloat16), "feat").astype(jnp.float32),
    )
    frob_part = jnp.sum(gram_a * gram_b)
    grad_na = (
        coef * jnp.dot(gram_b.astype(jnp.bfloat16), full_a, preferred_element_type=jnp.float32)
        + wide_b * factor
    )
    grad_nb = (
        coef * jnp.dot(gram_a.astype(jnp.bfloat16), full_b, preferred_element_type=jnp.float32)
        + wide_a * factor
    )
    stats = jnp.stack(
        [
            jnp.sum(grad_na, axis=0),
            jnp.sum(grad_nb, axis=0),
            jnp.sum(grad_na * hat_a, axis=0),
            jnp.sum(grad_nb * hat_b, axis=0),
        ]
    )
    back_total = lax.psum(stats, "img")
    share = LAMBDA * frob_part / (images * images) / feat_parts + diag_part / img_parts
    loss = lax.psum(share, ("img", "feat"))
    back_mean = back_total / images
    grad_pa = (rstd_ab[0] * (grad_na - back_mean[0] - hat_a * back_mean[2])).astype(jnp.bfloat16)
    grad_pb = (rstd_ab[1] * (grad_nb - back_mean[1] - hat_b * back_mean[3])).astype(jnp.bfloat16)
    both_grads = jnp.stack([grad_pa, grad_pb])
    partial_rows = lax.dot_general(
        both_grads, projection, (((2,), (1,)), ((), ())), preferred_element_type=jnp.float32
    )
    summed = lax.psum_scatter(
        partial_rows.astype(jnp.bfloat16), "feat", scatter_dimension=2, tiled=True
    ).astype(jnp.float32)
    return (loss, summed[0].astype(jnp.bfloat16), summed[1].astype(jnp.bfloat16))


def solution(mesh):
    in_specs = (P("img", None), P("img", None), P(None, "feat"))
    out_specs = (P(), P("img", "feat"), P("img", "feat"))
    return jax.shard_map(
        on_device, mesh=mesh, in_specs=in_specs, out_specs=out_specs, check_vma=False
    )
```

profile of v0, /device:TPU:1, one launch (start us, length us, event | category | flops | bytes accessed | tf_op | source)
XLA Modules:
  0.0 676.4 jit_solution(10856388306864929719)
XLA Ops:
  7.2 0.0 copy-start
  7.2 0.0 copy-start.7
  7.2 0.0 all-gather.3.cloned.1.call-start
  7.2 1.0 copy-done
  8.2 0.0 copy-start.1
  8.2 3.1 fusion.24
  11.3 0.0 copy-done.7
  11.3 0.4 copy-done.1
  11.7 0.7 fusion.23
  12.5 65.3 %psum.49 = f32[2,1024]{1,0:T(2,128)S(1)} all-reduce(f32[2,1024]{1,0:T(2,128)S(1)} %pad_maximum_fusion.1), channel_id=1, replica_groups=mesh['img'=32,'feat'=8] {'img'}, use_global_device_ids=true, to_apply=%region_2.0 | all-reduce | flops 2048 | bytes 16384 | tf_op jit(solution)/shard_map/psum | solution.py:22
  77.8 0.1 multiply_reduce_fusion.4
  77.9 0.1 multiply_reduce_fusion.3
  78.0 56.8 %psum.50 = f32[2,1024]{1,0:T(2,128)S(1)} all-reduce(f32[2,1024]{1,0:T(2,128)S(1)} %pad_maximum_fusion.2), channel_id=1, replica_groups=mesh['img'=32,'feat'=8] {'img'}, use_global_device_ids=true, to_apply=%region_5.0 | all-reduce | flops 2048 | bytes 16384 | tf_op jit(solution)/shard_map/psum | solution.py:26
  134.9 1.0 fusion.7
  135.9 0.0 all-gather.3.cloned.1.call-update
  135.9 0.0 all-gather.5.cloned.1.call-start
  135.9 0.7 all-gather.5.cloned.1.call-update
  136.6 0.0 copy-start.4
  136.6 0.0 all-reduce.3.cloned.1.call-start
  136.7 121.5 %all-gather.3.cloned.1.call-done = bf16[4096,1024]{1,0:T(8,128)(2,1)} async-done(((bf16[128,1024]{1,0:T(8,128)(2,1)}), bf16[4096,1024]{1,0:T(8,128)(2,1)}) %all-gather.3.cloned.1.call-update) | async-done | bytes 8388624 | tf_op jit(solution)/shard_map/all_gather | solution.py:41
  258.2 7.4 %convolution_convert_fusion.1 = bf16[128,4096]{1,0:T(8,128)(2,1)} fusion(bf16[128,1024]{1,0:T(8,128)(2,1)} %get-tuple-element.12, bf16[4096,1024]{1,0:T(8,128)(2,1)} %all-gather.3.cloned.1.call-done), kind=kOutput, calls=%fused_computation.1 | convolution fusion | flops 1074266112 | bytes 9699328 | tf_op jit(solution)/shard_map/dot_general | solution.py:11
  265.6 0.0 copy-start.5
  265.6 90.7 %all-gather.5.cloned.1.call-done = bf16[4096,1024]{1,0:T(8,128)(2,1)} async-done(((bf16[128,1024]{1,0:T(8,128)(2,1)}), bf16[4096,1024]{1,0:T(8,128)(2,1)}) %all-gather.5.cloned.1.call-update) | async-done | bytes 8388624 | tf_op jit(solution)/shard_map/all_gather | solution.py:42
  356.2 0.0 copy-done.4
  356.2 7.3 %convolution_convert_fusion = bf16[128,4096]{1,0:T(8,128)(2,1)} fusion(bf16[128,1024]{1,0:T(8,128)(2,1)S(1)} %copy-done.4, bf16[4096,1024]{1,0:T(8,128)(2,1)} %all-gather.5.cloned.1.call-done), kind=kOutput, calls=%fused_computation | convolution fusion | flops 1074266112 | bytes 9699328 | tf_op jit(solution)/shard_map/dot_general | solution.py:11
  363.5 0.0 all-reduce.3.cloned.1.call-update
  363.5 0.0 reduce-scatter.2.cloned.1.call-start
  363.6 57.6 %psum.53 = f32[1024]{0:T(1024)S(1)} all-reduce(f32[1024]{0:T(1024)S(1)} %get-tuple-element.11), channel_id=1, replica_groups=mesh['img'=32,'feat'=8] {'img'}, use_global_device_ids=true, to_apply=%region_10.0 | all-reduce | flops 1024 | bytes 8192 | tf_op jit(solution)/shard_map/psum | solution.py:38
  421.2 0.6 multiply_reduce_fusion.5
  421.8 8.8 %all-reduce.3.cloned.1.call-done = (bf16[128,4096]{1,0:T(8,128)(2,1)}, bf16[128,4096]{1,0:T(8,128)(2,1)}) async-done(((bf16[128,4096]{1,0:T(8,128)(2,1)}, bf16[128,4096]{1,0:T(8,128)(2,1)}), (bf16[128,4096]{1,0:T(8,128)(2,1)}, bf16[128,4096]{1,0:T(8,128)(2,1)})) %all-reduce.3.cloned.1.call-update) | async-done | bytes 2097168 | tf_op jit(solution)/shard_map/psum | solution.py:50
  430.6 0.0 copy-done.5
  430.6 0.0 copy-start.2
  430.6 6.0 fusion.17
  436.5 0.0 copy-done.2
  436.5 0.0 copy-start.6
  436.6 5.6 fusion.16
  442.2 115.4 %psum.55 = f32[4,1024]{1,0:T(4,128)S(1)} all-reduce(f32[4,1024]{1,0:T(4,128)S(1)} %pad_maximum_fusion), channel_id=1, replica_groups=mesh['img'=32,'feat'=8] {'img'}, use_global_device_ids=true, to_apply=%region_18.0 | all-reduce | flops 4096 | bytes 32768 | tf_op jit(solution)/shard_map/psum | solution.py:69
  557.6 0.0 copy-done.6
  557.7 1.3 fusion.13
  559.0 0.0 copy-start.3
  559.0 4.6 fusion.2
  563.5 0.0 reduce-scatter.2.cloned.1.call-update
  564.8 0.0 copy-done.3
  564.9 1.1 multiply_reduce_fusion
  566.7 101.7 %psum.54 = f32[]{:T(128)} all-reduce(f32[]{:T(128)S(6)} %add.33), channel_id=1, replica_groups=mesh['img'=32,'feat'=8] {'img','feat'}, use_global_device_ids=true, to_apply=%region_13.0 | all-reduce | flops 1 | bytes 8 | tf_op jit(solution)/shard_map/psum | solution.py:71
  668.3 0.0 reduce-scatter.2.cloned.1.call-done
  668.3 1.5 slice_bitcast_fusion
  (9 shorter events, 0.1 us)
Async XLA Ops:
  7.2 1.0 copy-start
  7.2 4.1 copy-start.7
  7.2 251.0 %all-gather.3.cloned.1.call-start = ((), (), s32[]{:S(2)}) async-start(), calls=%async_computation.1 | async-start | bytes 8650752 | tf_op jit(solution)/shard_map/all_gather | solution.py:41
  8.2 3.5 copy-start.1
  135.9 220.4 %all-gather.5.cloned.1.call-start = ((), (), s32[]{:S(2)}) async-start(), calls=%async_computation.2 | async-start | bytes 8650752 | tf_op jit(solution)/shard_map/all_gather | solution.py:42
  136.6 219.6 %copy-start.4 = (bf16[128,1024]{1,0:T(8,128)(2,1)S(1)}, bf16[128,1024]{1,0:T(8,128)(2,1)}, u32[]{:S(2)}) copy-start(bf16[128,1024]{1,0:T(8,128)(2,1)} %get-tuple-element.13) | copy-start | bytes 786436
  136.6 293.9 %all-reduce.3.cloned.1.call-start = ((), (), s32[]{:S(2)}) async-start(), calls=%async_computation.4 | async-start | bytes 4194304 | tf_op jit(solution)/shard_map/psum | solution.py:50
  265.6 165.0 %copy-start.5 = (bf16[128,1024]{1,0:T(8,128)(2,1)S(1)}, bf16[128,1024]{1,0:T(8,128)(2,1)}, u32[]{:S(2)}) copy-start(bf16[128,1024]{1,0:T(8,128)(2,1)} %get-tuple-element.12) | copy-start | bytes 786436
  363.5 304.8 %reduce-scatter.2.cloned.1.call-start = ((), (), s32[]{:S(2)}) async-start(), calls=%async_computation.3 | async-start | bytes 1179648 | tf_op jit(solution)/shard_map/reduce_scatter | solution.py:79
  430.6 6.0 copy-start.2
  436.5 121.1 %copy-start.6 = (f32[128,1024]{1,0:T(8,128)S(1)}, f32[128,1024]{1,0:T(8,128)}, u32[]{:S(2)}) copy-start(f32[128,1024]{1,0:T(8,128)} %get-tuple-element.29) | copy-start | bytes 1572868
  559.0 5.9 copy-start.3
Sparse Core Ops, SparseCore 0:
  136.0 122.1 all-gather.2
  260.8 95.4 all-gather.4
  363.6 66.8 all-reduce.2
  563.7 57.2 reduce-scatter.1
where the time goes:
time: 677 us; the launch traced here: 676 us
  blocking collectives  397 us (59%)
  waiting for transfers between devices  222 us (33%)
  matrix products  34.6 us (5%)
  between operations  15.9 us (2%)
    all_gather x1, waiting for transfers between devices, on_device(): lax.all_gather(norm_a, 'img', axis=0, tiled=True)  122 us
    psum x1, blocking collectives, on_device(): back_total = lax.psum(stats, 'img')  115 us
    psum x1, blocking collectives, on_device(): loss = lax.psum(share, ('img', 'feat'))  102 us
    all_gather x1, waiting for transfers between devices, on_device(): lax.all_gather(norm_b, 'img', axis=0, tiled=True)  90.7 us
    psum x1, blocking collectives, on_device(): lax.psum(jnp.stack([jnp.sum(proj_a, axis=0), jnp.sum(proj_b, axis=0)]), '...  65.3 us
    psum x1, blocking collectives, on_device(): corr = lax.psum(jnp.sum(wide_a * wide_b, axis=0), 'img') / images  57.6 us
    psum x1, blocking collectives, on_device(): lax.psum(jnp.stack([jnp.sum(center_a * center_a, axis=0), jnp.sum(center_...  56.8 us
    dot_general x2, matrix products, gram_rows(): lax.dot_general(local, full, (((1,), (1,)), ((), ())), preferred_element_...  14.6 us
  transfers between devices with their start and end apart: 4, of which 3 were waited for; matrix products, arithmetic and copies ran while one was open for 1% of the time, Pallas kernels for 0%

commit v1 on v0

v1 whole, which is shorter than its diff:
```python
import functools
import jax
import jax.numpy as jnp
from jax import lax
from jax.experimental import pallas as pl
from jax.experimental.pallas import tpu as pltpu
from jax.sharding import PartitionSpec as P

LAMBDA = 0.0051
EPSILON = 1e-05
MESH = pl.DeviceIdType.MESH
NZ, NX, NY = 8, 4, 4
F32, BF16 = jnp.float32, jnp.bfloat16
NEAR_Z = (1, 7, 2, 6, 3, 5, 4)
NEAR_4 = (1, 3, 2)


def remote(src, dst, send_sem, recv_sem, device):
    return pltpu.make_async_remote_copy(
        src_ref=src, dst_ref=dst, send_sem=send_sem, recv_sem=recv_sem,
        device_id=device, device_id_type=MESH,
    )


def dot_nt(a, b):
    return lax.dot_general(a, b, (((1,), (1,)), ((), ())), preferred_element_type=F32)


def dot_nn(a, b):
    return jnp.dot(a, b, preferred_element_type=F32)


def merge(parts, count):
    n = len(parts)
    ma = sum(p[0] for p in parts) * (1.0 / n)
    mb = sum(p[1] for p in parts) * (1.0 / n)
    da = [p[0] - ma for p in parts]
    db = [p[1] - mb for p in parts]
    saa = sum(p[2] for p in parts) + count * sum(d * d for d in da)
    sbb = sum(p[3] for p in parts) + count * sum(d * d for d in db)
    sab = sum(p[4] for p in parts) + count * sum(d * e for d, e in zip(da, db))
    return [ma, mb, saa, sbb, sab]


def kernel(
    va, vb, proj, loss_ref, ga_ref, gb_ref,
    vv, pw, hat, hr, grad, back,
    tp, txr, txs, tzr, tfull, mxl, mxr, mzs, mzr, mcorr,
    stx, stz, lcs, lcr, lys, lyr, la, lb,
    zcs, zcr, zys, zyr, zall, gsx, gsz,
    ocs, ocr, oys, oyr, lo, lorc, lo2, lory,
    in_sem, tx_s, tx_r, mx_s, mx_r, tz_s, tz_r, mz_s, mz_r, az_s, az_r, ax_s, ax_r,
    sx_s, sx_r, sz_s, sz_r, lc_s, lc_r, ly_s, ly_r, lay_s, lay_r, lac_s, lac_r,
    zc_s, zc_r, zy_s, zy_r, zay_s, zay_r, zac_s, zac_r, zby_s, zby_r, zbc_s, zbc_r,
    gx_s, gx_r, gz_s, gz_r, oc_s, oc_r, oy_s, oy_r, lo_s, lo_r,
):
    images = 128 * NZ * NX
    img, feat = lax.axis_index("img"), lax.axis_index("feat")
    z, x = lax.div(img, NX), lax.rem(img, NX)
    y, core = lax.div(feat, 2), lax.rem(feat, 2)
    zs = [lax.rem(z + d, NZ) for d in range(NZ)]
    xs = [lax.rem(x + d, NX) for d in range(NX)]
    ys = [lax.rem(y + d, NY) for d in range(NY)]
    yback = [lax.rem(y + NY - d, NY) for d in range(NY)]
    zback = [lax.rem(z + NZ - d, NZ) for d in range(NZ)]
    zdev = [(v * NX + x, feat) for v in zs]
    xdev = [(z * NX + v, feat) for v in xs]
    ydev = [(img, v * 2 + core) for v in ys]
    cdev = (img, y * 2 + 1 - core)

    loads = [
        pltpu.make_async_copy(va, vv.at[pl.ds(0, 128)], in_sem.at[0]),
        pltpu.make_async_copy(vb, vv.at[pl.ds(128, 128)], in_sem.at[1]),
        pltpu.make_async_copy(proj, pw, in_sem.at[2]),
    ]
    for cp in loads:
        cp.start()
    barrier = pltpu.get_barrier_semaphore()
    peers = zdev[1:] + xdev[1:] + ydev[1:] + [cdev]
    for peer in peers:
        pl.semaphore_signal(barrier, inc=1, device_id=peer, device_id_type=MESH)

    sent = []

    def send(src, dst, send_sem, recv_sem, device):
        cp = remote(src, dst, send_sem, recv_sem, device)
        cp.start()
        sent.append(cp)
        return cp

    loads[0].wait()
    loads[1].wait()
    bcols = vv[128:256, pl.ds(pl.multiple_of(feat * 256, 256), 256)].astype(F32)
    bmean = jnp.sum(bcols, axis=0, keepdims=True) * (1.0 / 128)
    ct = (bcols - bmean).T.astype(BF16)
    mxl[8:9, :] = bmean
    for i in range(8):
        acols = vv[0:128, i * 256:(i + 1) * 256].astype(F32)
        amean = jnp.sum(acols, axis=0, keepdims=True) * (1.0 / 128)
        mxl[i:i + 1, :] = amean
        tp[i] = dot_nn(ct, (acols - amean).astype(BF16)).astype(BF16)
    pl.semaphore_wait(barrier, len(peers))
    mx, tx = {}, {}
    for d in NEAR_4:
        mx[d] = send(mxl, mxr.at[d - 1], mx_s.at[d - 1], mx_r.at[d - 1], xdev[d])
    for d in NEAR_4:
        tx[d] = send(
            tp.at[:, pl.ds(pl.multiple_of(xs[d] * 64, 64), 64), :], txr.at[d - 1],
            tx_s.at[d - 1], tx_r.at[d - 1], xdev[d],
        )

    loads[2].wait()

    def project(n, carry):
        cols = pl.ds(pl.multiple_of(n * 256, 256), 256)
        pr = dot_nn(vv[...], pw[:, cols])
        hat[:, cols] = pr
        pa, pb = pr[0:128], pr[128:256]
        ma = jnp.sum(pa, axis=0, keepdims=True) * (1.0 / 128)
        mb = jnp.sum(pb, axis=0, keepdims=True) * (1.0 / 128)
        pa, pb = pa - ma, pb - mb
        stx[x, 0, :, cols] = ma
        stx[x, 1, :, cols] = mb
        stx[x, 2, :, cols] = jnp.sum(pa * pa, axis=0, keepdims=True)
        stx[x, 3, :, cols] = jnp.sum(pb * pb, axis=0, keepdims=True)
        stx[x, 4, :, cols] = jnp.sum(pa * pb, axis=0, keepdims=True)
        return carry

    lax.fori_loop(0, 4, project, 0)
    sx = {d: send(stx.at[x], stx.at[x], sx_s.at[d - 1], sx_r.at[d - 1], xdev[d]) for d in NEAR_4}
    for d in NEAR_4:
        sx[d].wait_recv()
    merged = merge([[stx[k, i] for i in range(5)] for k in range(NX)], 128.0)
    for i in range(5):
        stz[z, i] = merged[i]
    sz = {d: send(stz.at[z], stz.at[z], sz_s.at[d - 1], sz_r.at[d - 1], zdev[d]) for d in NEAR_Z}

    for d in NEAR_4:
        mx[d].wait_recv()
    for i in range(8):
        for r in range(4):
            am = mxl[i:i + 1, :] if r == 0 else mxr[r - 1, i:i + 1, :]
            bm = mxl[8:9, :] if r == 0 else mxr[r - 1, 8:9, :]
            mzs[i, 0, r:r + 1, :] = am
            mzs[i, 0, r + 4:r + 5, :] = am
            mzs[i, 1, r:r + 1, :] = bm
            mzs[i, 1, r + 4:r + 5, :] = bm
    mz, tz = {}, {}
    for d in NEAR_Z:
        mz[d] = send(mzs.at[zs[d]], mzr.at[d - 1], mz_s.at[d - 1], mz_r.at[d - 1], zdev[d])
    xrows = pl.ds(pl.multiple_of(x * 64, 64), 64)

    def z_scatter():
        for d in NEAR_4:
            tx[d].wait_recv()
        for i in range(8):
            total = tp[i, xrows, :].astype(F32)
            for k in range(3):
                total = total + txr[k, i].astype(F32)
            txs[i] = total.astype(BF16)
        for d in NEAR_Z:
            tz[d] = send(txs.at[zs[d]], tzr.at[d - 1], tz_s.at[d - 1], tz_r.at[d - 1], zdev[d])

    for d in NEAR_Z:
        sz[d].wait_recv()
    mean_a, mean_b, saa, sbb, sab = merge(
        [[stz[k, i] for i in range(5)] for k in range(NZ)], 128.0 * NX
    )
    rstd_a = lax.rsqrt(saa * (1.0 / images) + EPSILON)
    rstd_b = lax.rsqrt(sbb * (1.0 / images) + EPSILON)
    corr = sab * rstd_a * rstd_b * (1.0 / images)
    factor = -2.0 * (1.0 - corr) - 2.0 * LAMBDA * corr
    coef = 2.0 * LAMBDA / images
    diag = jnp.sum((1.0 - corr) ** 2 - LAMBDA * corr * corr, axis=1, keepdims=True)
    hat_a = (hat[0:128, :] - mean_a) * rstd_a
    hat[0:128, :] = hat_a
    hr[0:128, :] = (hat_a * rstd_a).astype(BF16)
    hat_b = (hat[128:256, :] - mean_b) * rstd_b
    hat[128:256, :] = hat_b
    hr[128:256, :] = (hat_b * rstd_b).astype(BF16)

    def feat_scatter(chunk, cs, cr, y_send, y_recv, cs_s, cs_r, ysem_s, ysem_r):
        cc, yc = {}, {}
        for d in (1, 3, 2, 0):
            cs[d] = chunk(ys[d] * 2 + 1 - core).astype(BF16)
            cc[d] = send(cs.at[d], cr.at[d], cs_s.at[d], cs_r.at[d], cdev)
        for d in NEAR_4:
            own = chunk(ys[d] * 2 + core)
            cc[d].wait_recv()
            y_send[d - 1] = (own + cr[d].astype(F32)).astype(BF16)
            yc[d] = send(y_send.at[d - 1], y_recv.at[d - 1], ysem_s.at[d - 1], ysem_r.at[d - 1], ydev[d])
        total = chunk(feat)
        cc[0].wait_recv()
        total = total + cr[0].astype(F32)

        def finish():
            out = total
            for d in NEAR_4:
                yc[d].wait_recv()
                out = out + y_recv[d - 1].astype(F32)
            return out

        return finish

    def feat_gather(at, y_s, y_r, c_s, c_r):
        yc = {d: send(at(feat), at(feat), y_s.at[d - 1], y_r.at[d - 1], ydev[d]) for d in NEAR_4}
        cc = {0: send(at(feat), at(feat), c_s.at[0], c_r.at[0], cdev)}

        def forward():
            for d in NEAR_4:
                yc[d].wait_recv()
                there = at(yback[d] * 2 + core)
                cc[d] = send(there, there, c_s.at[d], c_r.at[d], cdev)

        def finish():
            for d in range(4):
                cc[d].wait_recv()

        return forward, finish

    def rows_of_p(i):
        return pw[pl.ds(pl.multiple_of(i * 256, 256), 256), :]

    l_finish = feat_scatter(
        lambda i: dot_nt(hr[...], rows_of_p(i)), lcs, lcr, lys, lyr, lc_s, lc_r, ly_s, ly_r
    )
    z_scatter()

    total = l_finish()
    la[feat] = total[0:128].astype(BF16)
    lb[...] = total[128:256].astype(BF16)
    la_forward, la_finish = feat_gather(lambda i: la.at[i], lay_s, lay_r, lac_s, lac_r)
    for d in NEAR_Z:
        mz[d].wait_recv()
    am = jnp.concatenate([mzs[z, 0]] + [mzr[k, 0] for k in range(7)], axis=0)
    bm = jnp.concatenate([mzs[z, 1]] + [mzr[k, 1] for k in range(7)], axis=0)
    am = am - jnp.sum(am, axis=0, keepdims=True) * (1.0 / 64)
    bm = bm - jnp.sum(bm, axis=0, keepdims=True) * (1.0 / 64)
    mcorr[...] = dot_nn((bm * 64.0).T.astype(BF16), am.astype(BF16))
    total = txs[z].astype(F32) + mcorr[xrows, :]
    for d in NEAR_Z:
        tz[d].wait_recv()
        total = total + tzr[d - 1].astype(F32)
    tfull[z, xrows, :] = total.astype(BF16)
    mine = tfull.at[z, xrows, :]
    az = {d: send(mine, mine, az_s.at[d - 1], az_r.at[d - 1], zdev[d]) for d in NEAR_Z}
    ax = {}
    for e in NEAR_4:
        ax[0, e] = send(mine, mine, ax_s.at[0, e - 1], ax_r.at[0, e - 1], xdev[e])
    la_forward()
    for d in NEAR_Z:
        az[d].wait_recv()
        there = tfull.at[zback[d], xrows, :]
        for e in NEAR_4:
            ax[d, e] = send(there, there, ax_s.at[d, e - 1], ax_r.at[d, e - 1], xdev[e])
    la_finish()
    for d in (0,) + NEAR_Z:
        for e in NEAR_4:
            ax[d, e].wait_recv()

    za_finish = feat_scatter(
        lambda i: dot_nn(lb[...], tfull[i]), zcs, zcr, zys, zyr, zc_s, zc_r, zy_s, zy_r
    )
    zb = sum(dot_nt(la[i], tfull[i]) for i in range(8))
    zall[feat, 128:256, :] = zb.astype(BF16)
    zb_forward, zb_finish = feat_gather(
        lambda i: zall.at[i, pl.ds(128, 128), :], zby_s, zby_r, zbc_s, zbc_r
    )
    zall[feat, 0:128, :] = za_finish().astype(BF16)
    za_forward, za_finish2 = feat_gather(
        lambda i: zall.at[i, pl.ds(0, 128), :], zay_s, zay_r, zac_s, zac_r
    )
    zb_forward()
    za_forward()
    zb_finish()
    za_finish2()

    back[0] = rstd_a
    back[1] = rstd_b
    back[2] = factor

    def gradient(n, carry):
        cols = pl.ds(pl.multiple_of(n * 256, 256), 256)
        g = sum(dot_nn(zall[i], pw[i * 256:(i + 1) * 256, cols]) for i in range(8))
        ra, rb, fac = back[0, :, cols], back[1, :, cols], back[2, :, cols]
        ha, hb = hat[0:128, cols], hat[128:256, cols]
        qa = g[0:128] * ra
        na = coef * qa + hb * fac
        nb = coef * (g[128:256] * rb) + ha * fac
        grad[0:128, cols] = na
        grad[128:256, cols] = nb
        gsx[x, 0, :, cols] = jnp.sum(na, axis=0, keepdims=True)
        gsx[x, 1, :, cols] = jnp.sum(nb, axis=0, keepdims=True)
        gsx[x, 2, :, cols] = jnp.sum(na * ha, axis=0, keepdims=True)
        gsx[x, 3, :, cols] = jnp.sum(nb * hb, axis=0, keepdims=True)
        gsx[x, 4, :, cols] = jnp.sum(qa * ha, axis=0, keepdims=True)
        return carry

    lax.fori_loop(0, 4, gradient, 0)
    gx = {d: send(gsx.at[x], gsx.at[x], gx_s.at[d - 1], gx_r.at[d - 1], xdev[d]) for d in NEAR_4}
    for d in NEAR_4:
        gx[d].wait_recv()
    for i in range(5):
        gsz[z, i] = (gsx[0, i] + gsx[1, i]) + (gsx[2, i] + gsx[3, i])
    gz = {d: send(gsz.at[z], gsz.at[z], gz_s.at[d - 1], gz_r.at[d - 1], zdev[d]) for d in NEAR_Z}
    for d in NEAR_Z:
        gz[d].wait_recv()
    sums = [sum(gsz[k, i] for k in range(NZ)) for i in range(5)]
    means = [s * (1.0 / images) for s in sums[:4]]
    hr[0:128, :] = (rstd_a * (grad[0:128, :] - means[0] - hat[0:128, :] * means[2])).astype(BF16)
    hr[128:256, :] = (rstd_b * (grad[128:256, :] - means[1] - hat[128:256, :] * means[3])).astype(BF16)

    share = diag + (LAMBDA / (images * images)) * jnp.sum(sums[4], axis=1, keepdims=True)
    lo[...] = jnp.broadcast_to(share, (8, 128))
    lc = send(lo, lorc, lo_s.at[0], lo_r.at[0], cdev)
    o_finish = feat_scatter(
        lambda i: dot_nt(hr[...], rows_of_p(i)), ocs, ocr, oys, oyr, oc_s, oc_r, oy_s, oy_r
    )
    lc.wait_recv()
    pair = jnp.where(core == 0, lo[...] + lorc[...], lorc[...] + lo[...])
    lo2[...] = pair
    lly = {d: send(lo2, lory.at[y], lo_s.at[d], lo_r.at[d], ydev[d]) for d in NEAR_4}
    lory[y] = pair
    total = o_finish()
    ga_ref[...] = total[0:128].astype(BF16)
    gb_ref[...] = total[128:256].astype(BF16)
    for d in NEAR_4:
        lly[d].wait_recv()
    loss_ref[...] = (lory[0] + lory[1]) + (lory[2] + lory[3])
    for cp in sent:
        cp.wait_send()


def on_device(view_a, view_b, projection):
    dma = pltpu.SemaphoreType.DMA
    vmem = pltpu.VMEM
    scratch = [
        vmem((256, 2048), BF16), vmem((2048, 1024), BF16), vmem((256, 1024), F32),
        vmem((256, 1024), BF16), vmem((256, 1024), F32), vmem((3, 1, 1024), F32),
        vmem((8, 256, 256), BF16), vmem((3, 8, 64, 256), BF16), vmem((8, 64, 256), BF16),
        vmem((7, 64, 256), BF16), vmem((8, 256, 256), BF16),
        vmem((16, 256), F32), vmem((3, 16, 256), F32),
        vmem((8, 2, 8, 256), F32), vmem((7, 2, 8, 256), F32), vmem((256, 256), F32),
        vmem((4, 5, 1, 1024), F32), vmem((8, 5, 1, 1024), F32),
        vmem((4, 256, 256), BF16), vmem((4, 256, 256), BF16), vmem((3, 256, 256), BF16),
        vmem((3, 256, 256), BF16), vmem((8, 128, 256), BF16), vmem((128, 256), BF16),
        vmem((4, 128, 256), BF16), vmem((4, 128, 256), BF16), vmem((3, 128, 256), BF16),
        vmem((3, 128, 256), BF16), vmem((8, 256, 256), BF16),
        vmem((4, 5, 1, 1024), F32), vmem((8, 5, 1, 1024), F32),
        vmem((4, 256, 256), BF16), vmem((4, 256, 256), BF16), vmem((3, 256, 256), BF16),
        vmem((3, 256, 256), BF16),
        vmem((8, 128), F32), vmem((8, 128), F32), vmem((8, 128), F32), vmem((4, 8, 128), F32),
        dma((3,)),
    ]
    sizes = [
        (3,), (3,), (7,), (7,), (7,), (8, 3),
        (3,), (7,), (4,), (3,), (3,), (4,),
        (4,), (3,), (3,), (4,), (3,), (4,),
        (3,), (7,), (4,), (3,), (4,),
    ]
    for s in sizes:
        scratch += [dma(s), dma(s)]
    loss, ga, gb = pl.pallas_call(
        kernel,
        out_shape=(
            jax.ShapeDtypeStruct((8, 128), F32),
            jax.ShapeDtypeStruct((128, 256), BF16),
            jax.ShapeDtypeStruct((128, 256), BF16),
        ),
        in_specs=[pl.BlockSpec(memory_space=pl.ANY)] * 3,
        out_specs=[pl.BlockSpec(memory_space=pltpu.VMEM)] * 3,
        scratch_shapes=scratch,
        compiler_params=pltpu.CompilerParams(
            collective_id=0, has_side_effects=True, vmem_limit_bytes=48 * 1024 * 1024
        ),
        cost_estimate=pl.CostEstimate(flops=5 * 10**9, bytes_accessed=6 * 10**6, transcendentals=0),
        name="twins",
    )(view_a, view_b, projection)
    return loss[0, 0], ga, gb


def solution(mesh):
    in_specs = (P("img", None), P("img", None), P(None, "feat"))
    out_specs = (P(), P("img", "feat"), P("img", "feat"))
    return jax.shard_map(
        on_device, mesh=mesh, in_specs=in_specs, out_specs=out_specs, check_vma=False
    )
```

time: 677 us -> 107 us (0.16)
  blocking collectives: 397 us -> 0 us
  waiting for transfers between devices: 222 us -> 0 us
  Pallas kernels: 0 us -> 99.7 us
  matrix products: 34.6 us -> 0 us
  between operations: 15.9 us -> 0.65 us
    psum x5 -> x0, blocking collectives: 397 us -> none  [the longest x1 115 us: on_device(): back_total = lax.psum(stats, 'img')]
    all_gather x2 -> x0, waiting for transfers between devices: 212 us -> none  [the longest x1 122 us: on_device(): lax.all_gather(norm_a, 'img', axis=0, tiled=True)]
    pallas_call x0 -> x1, Pallas kernels: none -> 99.7 us  [on_device(): pl.pallas_call(kernel, out_shape=(jax.ShapeDtypeStruct((8, 128), F32), ja...]
    dot_general x7 -> x0, matrix products: 34.6 us -> none  [the longest x2 14.6 us: gram_rows(): lax.dot_general(local, full, (((1,), (1,)), ((), ())), preferred_element_...]
    psum x1 -> x0, waiting for transfers between devices: 8.79 us -> none  [on_device(): lax.psum(part_b.astype(jnp.bfloat16), 'feat').astype(jnp.float32)]
  transfers between devices with their start and end apart: 4 -> 0, of which waited for: 3 -> 0; matrix products, arithmetic and copies ran while one was open for 1% -> 0% of each run, Pallas kernels for 0% -> 0%
where the time goes in v1:
time: 107 us; the launch traced here: 106 us
  Pallas kernels  99.7 us (93%)
  local copies, waits for them, and re-layouts  6.03 us (6%)
    pallas_call x1, Pallas kernels, on_device(): pl.pallas_call(kernel, out_shape=(jax.ShapeDtypeStruct((8, 128), F32), ja...  99.7 us
    unnamed x8, local copies, waits for them, and re-layouts  5.52 us

profile of v1, /device:TPU:1, one launch (start us, length us, event | category | flops | bytes accessed | tf_op | source)
XLA Modules:
  0.0 106.4 jit_solution(16170106739764205403)
XLA Ops:
  0.6 0.0 copy-start
  0.6 2.2 %copy-done = bf16[2048,1024]{1,0:T(8,128)(2,1)S(1)} copy-done((bf16[2048,1024]{1,0:T(8,128)(2,1)S(1)}, bf16[2048,1024]{1,0:T(8,128)(2,1)}, u32[]{:S(2)}) %copy-start) | copy-done | bytes 4194328
  2.8 0.0 copy-start.1
  2.8 1.0 copy-done.1
  3.9 0.0 copy-start.2
  3.9 1.0 copy-done.2
  4.9 99.7 %twins.1 = (f32[8,128]{1,0:T(8,128)S(1)}, bf16[128,256]{1,0:T(8,128)(2,1)S(1)}, bf16[128,256]{1,0:T(8,128)(2,1)S(1)}) custom-call(bf16[128,2048]{1,0:T(8,128)(2,1)S(1)} %copy-done.1, bf16[128,2048]{1,0:T(8,128)(2,1)S(1)} %copy-done.2, bf16[2048,1024]{1,0:T(8,128)(2,1)S(1)} %copy-done), custom_call_target="tpu_custom_call" | custom-call | flops 5000000000 | bytes 6000000 | tf_op jit(solution)/shard_map/twins/pallas_call | solution.py:363
  104.7 0.5 slice.3
  105.2 0.6 copy.8
  105.8 0.6 copy.9
Async XLA Ops:
  0.6 2.2 %copy-start = (bf16[2048,1024]{1,0:T(8,128)(2,1)S(1)}, bf16[2048,1024]{1,0:T(8,128)(2,1)}, u32[]{:S(2)}) copy-start(bf16[2048,1024]{1,0:T(8,128)(2,1)} %proj.1) | copy-start | bytes 12582916
  2.8 1.0 copy-start.1
  3.9 1.0 copy-start.2

commit v2 on v1

--- a/solution.py
+++ b/solution.py
@@ -43,13 +43,13 @@
 
 
 def kernel(
-    va, vb, proj, loss_ref, ga_ref, gb_ref,
+    va, vb, proj, loss_ref, grads_ref,
     vv, pw, hat, hr, grad, back,
-    tp, txr, txs, tzr, tfull, mxl, mxr, mzs, mzr, mcorr,
+    xa, xb, tp, tzr, tfull, mz, mcorr,
     stx, stz, lcs, lcr, lys, lyr, la, lb,
     zcs, zcr, zys, zyr, zall, gsx, gsz,
     ocs, ocr, oys, oyr, lo, lorc, lo2, lory,
-    in_sem, tx_s, tx_r, mx_s, mx_r, tz_s, tz_r, mz_s, mz_r, az_s, az_r, ax_s, ax_r,
+    in_sem, xa_s, xa_r, xb_s, xb_r, xc_s, xc_r, tz_s, tz_r, mz_s, mz_r, az_s, az_r, ax_s, ax_r,
     sx_s, sx_r, sz_s, sz_r, lc_s, lc_r, ly_s, ly_r, lay_s, lay_r, lac_s, lac_r,
     zc_s, zc_r, zy_s, zy_r, zay_s, zay_r, zac_s, zac_r, zby_s, zby_r, zbc_s, zbc_r,
     gx_s, gx_r, gz_s, gz_r, oc_s, oc_r, oy_s, oy_r, lo_s, lo_r,
@@ -61,6 +61,7 @@
     zs = [lax.rem(z + d, NZ) for d in range(NZ)]
     xs = [lax.rem(x + d, NX) for d in range(NX)]
     ys = [lax.rem(y + d, NY) for d in range(NY)]
+    xback = [lax.rem(x + NX - d, NX) for d in range(NX)]
     yback = [lax.rem(y + NY - d, NY) for d in range(NY)]
     zback = [lax.rem(z + NZ - d, NZ) for d in range(NZ)]
     zdev = [(v * NX + x, feat) for v in zs]
@@ -88,27 +89,14 @@
         sent.append(cp)
         return cp
 
+    def cols256(i):
+        return pl.ds(pl.multiple_of(i * 256, 256), 256)
+
     loads[0].wait()
     loads[1].wait()
-    bcols = vv[128:256, pl.ds(pl.multiple_of(feat * 256, 256), 256)].astype(F32)
-    bmean = jnp.sum(bcols, axis=0, keepdims=True) * (1.0 / 128)
-    ct = (bcols - bmean).T.astype(BF16)
-    mxl[8:9, :] = bmean
-    for i in range(8):
-        acols = vv[0:128, i * 256:(i + 1) * 256].astype(F32)
-        amean = jnp.sum(acols, axis=0, keepdims=True) * (1.0 / 128)
-        mxl[i:i + 1, :] = amean
-        tp[i] = dot_nn(ct, (acols - amean).astype(BF16)).astype(BF16)
-    pl.semaphore_wait(barrier, len(peers))
-    mx, tx = {}, {}
-    for d in NEAR_4:
-        mx[d] = send(mxl, mxr.at[d - 1], mx_s.at[d - 1], mx_r.at[d - 1], xdev[d])
-    for d in NEAR_4:
-        tx[d] = send(
-            tp.at[:, pl.ds(pl.multiple_of(xs[d] * 64, 64), 64), :], txr.at[d - 1],
-            tx_s.at[d - 1], tx_r.at[d - 1], xdev[d],
-        )
-
+    xa[0, x] = vv[0:128, cols256(x * 2)]
+    xa[1, x] = vv[0:128, cols256(x * 2 + 1)]
+    xb[x] = vv[128:256, cols256(feat)]
     loads[2].wait()
 
     def project(n, carry):
@@ -127,7 +115,20 @@
         return carry
 
     lax.fori_loop(0, 4, project, 0)
+    pl.semaphore_wait(barrier, len(peers))
     sx = {d: send(stx.at[x], stx.at[x], sx_s.at[d - 1], sx_r.at[d - 1], xdev[d]) for d in NEAR_4}
+
+    xac, xbc, xcc = {}, {}, {}
+    for d in (2, 1, 3):
+        xac[d] = send(
+            vv.at[pl.ds(0, 128), cols256(xs[d] * 2 + core)], xa.at[core, x],
+            xa_s.at[d - 1], xa_r.at[d - 1], xdev[d],
+        )
+        xbc[d] = send(
+            vv.at[pl.ds(128, 128), cols256(feat)], xb.at[x],
+            xb_s.at[d - 1], xb_r.at[d - 1], xdev[d],
+        )
+
     for d in NEAR_4:
         sx[d].wait_recv()
     merged = merge([[stx[k, i] for i in range(5)] for k in range(NX)], 128.0)
@@ -136,30 +137,30 @@
     sz = {d: send(stz.at[z], stz.at[z], sz_s.at[d - 1], sz_r.at[d - 1], zdev[d]) for d in NEAR_Z}
 
     for d in NEAR_4:
-        mx[d].wait_recv()
-    for i in range(8):
-        for r in range(4):
-            am = mxl[i:i + 1, :] if r == 0 else mxr[r - 1, i:i + 1, :]
-            bm = mxl[8:9, :] if r == 0 else mxr[r - 1, 8:9, :]
-            mzs[i, 0, r:r + 1, :] = am
-            mzs[i, 0, r + 4:r + 5, :] = am
-            mzs[i, 1, r:r + 1, :] = bm
-            mzs[i, 1, r + 4:r + 5, :] = bm
-    mz, tz = {}, {}
+        xac[d].wait_recv()
+        there = xa.at[core, xback[d]]
+        xcc[d] = send(there, there, xc_s.at[d - 1], xc_r.at[d - 1], cdev)
+
+    for d in NEAR_4:
+        xbc[d].wait_recv()
+    bcols = xb[...].reshape(512, 256).astype(F32)
+    bmean = jnp.sum(bcols, axis=0, keepdims=True) * (1.0 / 512)
+    ct = (bcols - bmean).T.astype(BF16)
+    mz[z, 2] = bmean
+    for d in NEAR_4:
+        xcc[d].wait_recv()
+    for h in range(2):
+        acols = xa[h].reshape(512, 256).astype(F32)
+        amean = jnp.sum(acols, axis=0, keepdims=True) * (1.0 / 512)
+        mz[z, h] = amean
+        tp[h] = dot_nn(ct, (acols - amean).astype(BF16)).astype(BF16)
+    mzc, tz = {}, {}
     for d in NEAR_Z:
-        mz[d] = send(mzs.at[zs[d]], mzr.at[d - 1], mz_s.at[d - 1], mz_r.at[d - 1], zdev[d])
-    xrows = pl.ds(pl.multiple_of(x * 64, 64), 64)
-
-    def z_scatter():
-        for d in NEAR_4:
-            tx[d].wait_recv()
-        for i in range(8):
-            total = tp[i, xrows, :].astype(F32)
-            for k in range(3):
-                total = total + txr[k, i].astype(F32)
-            txs[i] = total.astype(BF16)
-        for d in NEAR_Z:
-            tz[d] = send(txs.at[zs[d]], tzr.at[d - 1], tz_s.at[d - 1], tz_r.at[d - 1], zdev[d])
+        tz[d] = send(
+            tp.at[:, pl.ds(pl.multiple_of(zs[d] * 32, 32), 32), :], tzr.at[d - 1],
+            tz_s.at[d - 1], tz_r.at[d - 1], zdev[d],
+        )
+        mzc[d] = send(mz.at[z], mz.at[z], mz_s.at[d - 1], mz_r.at[d - 1], zdev[d])
 
     for d in NEAR_Z:
         sz[d].wait_recv()
@@ -179,16 +180,30 @@
     hat[128:256, :] = hat_b
     hr[128:256, :] = (hat_b * rstd_b).astype(BF16)
 
-    def feat_scatter(chunk, cs, cr, y_send, y_recv, cs_s, cs_r, ysem_s, ysem_r):
+    def feat_scatter(chunk, cs, cr, y_send, y_recv, cs_s, cs_r, ysem_s, ysem_r, between=None):
         cc, yc = {}, {}
-        for d in (1, 3, 2, 0):
+
+        def other(d):
             cs[d] = chunk(ys[d] * 2 + 1 - core).astype(BF16)
             cc[d] = send(cs.at[d], cr.at[d], cs_s.at[d], cs_r.at[d], cdev)
-        for d in NEAR_4:
-            own = chunk(ys[d] * 2 + core)
+
+        def own(d):
+            mine = chunk(ys[d] * 2 + core)
             cc[d].wait_recv()
-            y_send[d - 1] = (own + cr[d].astype(F32)).astype(BF16)
+            y_send[d - 1] = (mine + cr[d].astype(F32)).astype(BF16)
             yc[d] = send(y_send.at[d - 1], y_recv.at[d - 1], ysem_s.at[d - 1], ysem_r.at[d - 1], ydev[d])
+
+        other(2)
+        other(1)
+        other(3)
+        if between is not None:
+            other(0)
+            between()
+        own(2)
+        own(1)
+        own(3)
+        if between is None:
+            other(0)
         total = chunk(feat)
         cc[0].wait_recv()
         total = total + cr[0].astype(F32)
@@ -224,45 +239,52 @@
     l_finish = feat_scatter(
         lambda i: dot_nt(hr[...], rows_of_p(i)), lcs, lcr, lys, lyr, lc_s, lc_r, ly_s, ly_r
     )
-    z_scatter()
-
+    for d in NEAR_Z:
+        mzc[d].wait_recv()
+    am = [jnp.concatenate([mz[k, i] for k in range(NZ)], axis=0) for i in range(3)]
+    am = [m - jnp.sum(m, axis=0, keepdims=True) * (1.0 / NZ) for m in am]
+    bm = (am[2] * 512.0).T.astype(BF16)
+    zrows = pl.ds(pl.multiple_of(z * 32, 32), 32)
+    for h in range(2):
+        mcorr[h] = dot_nn(bm, am[h].astype(BF16))
+    total = tp[:, zrows, :].astype(F32) + mcorr[:, zrows, :]
+    for d in NEAR_Z:
+        tz[d].wait_recv()
+        total = total + tzr[d - 1].astype(F32)
+    tfull[pl.ds(2 * x, 2), zrows, :] = total.astype(BF16)
+    mine = tfull.at[pl.ds(2 * x, 2), zrows, :]
+    az = {d: send(mine, mine, az_s.at[d - 1], az_r.at[d - 1], zdev[d]) for d in NEAR_Z}
+    ax = {}
+    for e in NEAR_4:
+        ax[0, e] = send(mine, mine, ax_s.at[0, e - 1], ax_r.at[0, e - 1], xdev[e])
+
+    def forward(zset):
+        for d in zset:
+            az[d].wait_recv()
+            there = tfull.at[pl.ds(2 * x, 2), pl.ds(pl.multiple_of(zback[d] * 32, 32), 32), :]
+            for e in NEAR_4:
+                ax[d, e] = send(there, there, ax_s.at[d, e - 1], ax_r.at[d, e - 1], xdev[e])
+
+    forward((1, 7))
     total = l_finish()
     la[feat] = total[0:128].astype(BF16)
     lb[...] = total[128:256].astype(BF16)
     la_forward, la_finish = feat_gather(lambda i: la.at[i], lay_s, lay_r, lac_s, lac_r)
-    for d in NEAR_Z:
-        mz[d].wait_recv()
-    am = jnp.concatenate([mzs[z, 0]] + [mzr[k, 0] for k in range(7)], axis=0)
-    bm = jnp.concatenate([mzs[z, 1]] + [mzr[k, 1] for k in range(7)], axis=0)
-    am = am - jnp.sum(am, axis=0, keepdims=True) * (1.0 / 64)
-    bm = bm - jnp.sum(bm, axis=0, keepdims=True) * (1.0 / 64)
-    mcorr[...] = dot_nn((bm * 64.0).T.astype(BF16), am.astype(BF16))
-    total = txs[z].astype(F32) + mcorr[xrows, :]
-    for d in NEAR_Z:
-        tz[d].wait_recv()
-        total = total + tzr[d - 1].astype(F32)
-    tfull[z, xrows, :] = total.astype(BF16)
-    mine = tfull.at[z, xrows, :]
-    az = {d: send(mine, mine, az_s.at[d - 1], az_r.at[d - 1], zdev[d]) for d in NEAR_Z}
-    ax = {}
-    for e in NEAR_4:
-        ax[0, e] = send(mine, mine, ax_s.at[0, e - 1], ax_r.at[0, e - 1], xdev[e])
+    forward((2, 6))
     la_forward()
-    for d in NEAR_Z:
-        az[d].wait_recv()
-        there = tfull.at[zback[d], xrows, :]
-        for e in NEAR_4:
-            ax[d, e] = send(there, there, ax_s.at[d, e - 1], ax_r.at[d, e - 1], xdev[e])
+    forward((3, 5, 4))
     la_finish()
     for d in (0,) + NEAR_Z:
         for e in NEAR_4:
             ax[d, e].wait_recv()
 
+    def gram_b():
+        zb = sum(dot_nt(la[i], tfull[i]) for i in range(8))
+        zall[feat, 128:256, :] = zb.astype(BF16)
+
     za_finish = feat_scatter(
-        lambda i: dot_nn(lb[...], tfull[i]), zcs, zcr, zys, zyr, zc_s, zc_r, zy_s, zy_r
-    )
-    zb = sum(dot_nt(la[i], tfull[i]) for i in range(8))
-    zall[feat, 128:256, :] = zb.astype(BF16)
+        lambda i: dot_nn(lb[...], tfull[i]), zcs, zcr, zys, zyr, zc_s, zc_r, zy_s, zy_r, gram_b
+    )
     zb_forward, zb_finish = feat_gather(
         lambda i: zall.at[i, pl.ds(128, 128), :], zby_s, zby_r, zbc_s, zbc_r
     )
@@ -322,8 +344,7 @@
     lly = {d: send(lo2, lory.at[y], lo_s.at[d], lo_r.at[d], ydev[d]) for d in NEAR_4}
     lory[y] = pair
     total = o_finish()
-    ga_ref[...] = total[0:128].astype(BF16)
-    gb_ref[...] = total[128:256].astype(BF16)
+    grads_ref[...] = total.astype(BF16)
     for d in NEAR_4:
         lly[d].wait_recv()
     loss_ref[...] = (lory[0] + lory[1]) + (lory[2] + lory[3])
@@ -337,10 +358,9 @@
     scratch = [
         vmem((256, 2048), BF16), vmem((2048, 1024), BF16), vmem((256, 1024), F32),
         vmem((256, 1024), BF16), vmem((256, 1024), F32), vmem((3, 1, 1024), F32),
-        vmem((8, 256, 256), BF16), vmem((3, 8, 64, 256), BF16), vmem((8, 64, 256), BF16),
-        vmem((7, 64, 256), BF16), vmem((8, 256, 256), BF16),
-        vmem((16, 256), F32), vmem((3, 16, 256), F32),
-        vmem((8, 2, 8, 256), F32), vmem((7, 2, 8, 256), F32), vmem((256, 256), F32),
+        vmem((2, 4, 128, 256), BF16), vmem((4, 128, 256), BF16), vmem((2, 256, 256), BF16),
+        vmem((7, 2, 32, 256), BF16), vmem((8, 256, 256), BF16),
+        vmem((8, 3, 1, 256), F32), vmem((2, 256, 256), F32),
         vmem((4, 5, 1, 1024), F32), vmem((8, 5, 1, 1024), F32),
         vmem((4, 256, 256), BF16), vmem((4, 256, 256), BF16), vmem((3, 256, 256), BF16),
         vmem((3, 256, 256), BF16), vmem((8, 128, 256), BF16), vmem((128, 256), BF16),
@@ -353,30 +373,29 @@
         dma((3,)),
     ]
     sizes = [
-        (3,), (3,), (7,), (7,), (7,), (8, 3),
+        (3,), (3,), (3,), (7,), (7,), (7,), (8, 3),
         (3,), (7,), (4,), (3,), (3,), (4,),
         (4,), (3,), (3,), (4,), (3,), (4,),
         (3,), (7,), (4,), (3,), (4,),
     ]
     for s in sizes:
         scratch += [dma(s), dma(s)]
-    loss, ga, gb = pl.pallas_call(
+    loss, grads = pl.pallas_call(
         kernel,
         out_shape=(
             jax.ShapeDtypeStruct((8, 128), F32),
-            jax.ShapeDtypeStruct((128, 256), BF16),
-            jax.ShapeDtypeStruct((128, 256), BF16),
+            jax.ShapeDtypeStruct((256, 256), BF16),
         ),
-        in_specs=[pl.BlockSpec(memory_space=pl.ANY)] * 3,
-        out_specs=[pl.BlockSpec(memory_space=pltpu.VMEM)] * 3,
+        in_specs=[pl.BlockSpec(memory_space=pltpu.HBM)] * 3,
+        out_specs=[pl.BlockSpec(memory_space=pltpu.VMEM)] * 2,
         scratch_shapes=scratch,
         compiler_params=pltpu.CompilerParams(
-            collective_id=0, has_side_effects=True, vmem_limit_bytes=48 * 1024 * 1024
+            collective_id=0, has_side_effects=True, vmem_limit_bytes=63 * 1024 * 1024
         ),
         cost_estimate=pl.CostEstimate(flops=5 * 10**9, bytes_accessed=6 * 10**6, transcendentals=0),
         name="twins",
     )(view_a, view_b, projection)
-    return loss[0, 0], ga, gb
+    return loss[0, 0], grads[0:128], grads[128:256]
 
 
 def solution(mesh):

time: 107 us -> 91.5 us (0.86)
  Pallas kernels: 99.7 us -> 88 us
  local copies, waits for them, and re-layouts: 6.03 us -> 2.71 us
    pallas_call x1, Pallas kernels: 99.7 us -> 88 us  [on_device(): pl.pallas_call(kernel, out_shape=(jax.ShapeDtypeStruct((8, 128), F32), ja...]
    unnamed x8 -> x0, local copies, waits for them, and re-layouts: 5.52 us -> none
    slice x1 -> x2, local copies, waits for them, and re-layouts: 0.51 us -> 2.71 us  [on_device(): return (loss[0, 0], grads[0:128], grads[128:256])]
where the time goes in v2:
time: 91.5 us; the launch traced here: 91.3 us
  Pallas kernels  88 us (96%)
  local copies, waits for them, and re-layouts  2.71 us (3%)
    pallas_call x1, Pallas kernels, on_device(): pl.pallas_call(kernel, out_shape=(jax.ShapeDtypeStruct((8, 128), F32), ja...  88 us
    slice x2, local copies, waits for them, and re-layouts, on_device(): return (loss[0, 0], grads[0:128], grads[128:256])  2.71 us

profile of v2, /device:TPU:1, one launch (start us, length us, event | category | flops | bytes accessed | tf_op | source)
XLA Modules:
  0.0 91.3 jit_solution(18416356645331925586)
XLA Ops:
  0.6 88.0 %twins.1 = (f32[8,128]{1,0:T(8,128)}, bf16[256,256]{1,0:T(8,128)(2,1)}) custom-call(bf16[128,2048]{1,0:T(8,128)(2,1)} %va.1, bf16[128,2048]{1,0:T(8,128)(2,1)} %vb.1, bf16[2048,1024]{1,0:T(8,128)(2,1)} %proj.1), custom_call_target="tpu_custom_call" | custom-call | flops 5000000000 | bytes 6000000 | tf_op jit(solution)/shard_map/twins/pallas_call | solution.py:383
  88.6 1.2 %slice.9 = f32[1,1]{1,0:T(1,128)} slice(f32[8,128]{1,0:T(8,128)} %get-tuple-element.5), slice={[0:1], [0:1]} | slice | bytes 8 | tf_op jit(solution)/shard_map/slice | solution.py:398
  89.8 1.5 %fusion = (bf16[128,256]{1,0:T(8,128)(2,1)}, bf16[128,256]{1,0:T(8,128)(2,1)}) fusion(bf16[256,256]{1,0:T(8,128)(2,1)} %get-tuple-element.6), kind=kLoop, calls=%fused_computation | loop fusion | bytes 262144 | tf_op jit(solution)/shard_map/slice | solution.py:398

commit v3 on v2

--- a/solution.py
+++ b/solution.py
@@ -47,12 +47,12 @@
     vv, pw, hat, hr, grad, back,
     xa, xb, tp, tzr, tfull, mz, mcorr,
     stx, stz, lcs, lcr, lys, lyr, la, lb,
-    zcs, zcr, zys, zyr, zall, gsx, gsz,
-    ocs, ocr, oys, oyr, lo, lorc, lo2, lory,
+    zcs, zcr, zys, zyr, zown, zall, gax, gaz, gbx, gbz,
+    ocs, ocr, oys, oyr, pcs, pcr, pys, pyr, lo, lorc, lo2, lory,
     in_sem, xa_s, xa_r, xb_s, xb_r, xc_s, xc_r, tz_s, tz_r, mz_s, mz_r, az_s, az_r, ax_s, ax_r,
     sx_s, sx_r, sz_s, sz_r, lc_s, lc_r, ly_s, ly_r, lay_s, lay_r, lac_s, lac_r,
     zc_s, zc_r, zy_s, zy_r, zay_s, zay_r, zac_s, zac_r, zby_s, zby_r, zbc_s, zbc_r,
-    gx_s, gx_r, gz_s, gz_r, oc_s, oc_r, oy_s, oy_r, lo_s, lo_r,
+    gax_s, gax_r, gaz_s, gaz_r, gbx_s, gbx_r, gbz_s, gbz_r, oc_s, oc_r, oy_s, oy_r, pc_s, pc_r, py_s, py_r, lo_s, lo_r,
 ):
     images = 128 * NZ * NX
     img, feat = lax.axis_index("img"), lax.axis_index("feat")
@@ -92,11 +92,24 @@
     def cols256(i):
         return pl.ds(pl.multiple_of(i * 256, 256), 256)
 
+    pl.semaphore_wait(barrier, len(peers))
+    xac, xbc, xcc = {}, {}, {}
+    for d in (2, 1, 3):
+        xac[d] = send(
+            va.at[:, cols256(xs[d] * 2 + core)], xa.at[core, x],
+            xa_s.at[d - 1], xa_r.at[d - 1], xdev[d],
+        )
+        xbc[d] = send(
+            vb.at[:, cols256(feat)], xb.at[x],
+            xb_s.at[d - 1], xb_r.at[d - 1], xdev[d],
+        )
+
     loads[0].wait()
     loads[1].wait()
     xa[0, x] = vv[0:128, cols256(x * 2)]
     xa[1, x] = vv[0:128, cols256(x * 2 + 1)]
     xb[x] = vv[128:256, cols256(feat)]
+
     loads[2].wait()
 
     def project(n, carry):
@@ -115,31 +128,18 @@
         return carry
 
     lax.fori_loop(0, 4, project, 0)
-    pl.semaphore_wait(barrier, len(peers))
     sx = {d: send(stx.at[x], stx.at[x], sx_s.at[d - 1], sx_r.at[d - 1], xdev[d]) for d in NEAR_4}
 
-    xac, xbc, xcc = {}, {}, {}
-    for d in (2, 1, 3):
-        xac[d] = send(
-            vv.at[pl.ds(0, 128), cols256(xs[d] * 2 + core)], xa.at[core, x],
-            xa_s.at[d - 1], xa_r.at[d - 1], xdev[d],
-        )
-        xbc[d] = send(
-            vv.at[pl.ds(128, 128), cols256(feat)], xb.at[x],
-            xb_s.at[d - 1], xb_r.at[d - 1], xdev[d],
-        )
-
+    for d in NEAR_4:
+        xac[d].wait_recv()
+        there = xa.at[core, xback[d]]
+        xcc[d] = send(there, there, xc_s.at[d - 1], xc_r.at[d - 1], cdev)
     for d in NEAR_4:
         sx[d].wait_recv()
     merged = merge([[stx[k, i] for i in range(5)] for k in range(NX)], 128.0)
     for i in range(5):
         stz[z, i] = merged[i]
     sz = {d: send(stz.at[z], stz.at[z], sz_s.at[d - 1], sz_r.at[d - 1], zdev[d]) for d in NEAR_Z}
-
-    for d in NEAR_4:
-        xac[d].wait_recv()
-        there = xa.at[core, xback[d]]
-        xcc[d] = send(there, there, xc_s.at[d - 1], xc_r.at[d - 1], cdev)
 
     for d in NEAR_4:
         xbc[d].wait_recv()
@@ -180,7 +180,7 @@
     hat[128:256, :] = hat_b
     hr[128:256, :] = (hat_b * rstd_b).astype(BF16)
 
-    def feat_scatter(chunk, cs, cr, y_send, y_recv, cs_s, cs_r, ysem_s, ysem_r, between=None):
+    def feat_scatter(chunk, cs, cr, y_send, y_recv, cs_s, cs_r, ysem_s, ysem_r):
         cc, yc = {}, {}
 
         def other(d):
@@ -196,14 +196,10 @@
         other(2)
         other(1)
         other(3)
-        if between is not None:
-            other(0)
-            between()
         own(2)
         own(1)
         own(3)
-        if between is None:
-            other(0)
+        other(0)
         total = chunk(feat)
         cc[0].wait_recv()
         total = total + cr[0].astype(F32)
@@ -258,96 +254,165 @@
     for e in NEAR_4:
         ax[0, e] = send(mine, mine, ax_s.at[0, e - 1], ax_r.at[0, e - 1], xdev[e])
 
+    def piece(d, e):
+        there = tfull.at[pl.ds(2 * x, 2), pl.ds(pl.multiple_of(zback[d] * 32, 32), 32), :]
+        ax[d, e] = send(there, there, ax_s.at[d, e - 1], ax_r.at[d, e - 1], xdev[e])
+
     def forward(zset):
         for d in zset:
             az[d].wait_recv()
-            there = tfull.at[pl.ds(2 * x, 2), pl.ds(pl.multiple_of(zback[d] * 32, 32), 32), :]
             for e in NEAR_4:
-                ax[d, e] = send(there, there, ax_s.at[d, e - 1], ax_r.at[d, e - 1], xdev[e])
+                piece(d, e)
 
     forward((1, 7))
     total = l_finish()
     la[feat] = total[0:128].astype(BF16)
     lb[...] = total[128:256].astype(BF16)
     la_forward, la_finish = feat_gather(lambda i: la.at[i], lay_s, lay_r, lac_s, lac_r)
-    forward((2, 6))
+    forward((2, 6, 3, 5, 4))
+
+    zcc = {}
+
+    def za_other(e):
+        zcs[e] = dot_nn(lb[...], tfull[xback[e] * 2 + 1 - core]).astype(BF16)
+        zcc[e] = send(zcs.at[e], zcr.at[e], zc_s.at[e], zc_r.at[e], cdev)
+
+    def za_copy(slot, there):
+        return remote(
+            zys.at[slot], zyr.at[slot], zy_s.at[slot], zy_r.at[slot], (img, there * 2 + core)
+        )
+
+    def za_own(e):
+        there = xback[e]
+        total = dot_nn(lb[...], tfull[there * 2 + core])
+        zcc[e].wait_recv()
+        total = total + zcr[e].astype(F32)
+        slot = jnp.maximum(lax.rem(there - y + NY, NY) - 1, 0)
+
+        @pl.when(there == y)
+        def _():
+            zown[...] = total
+
+        @pl.when(there != y)
+        def _():
+            zys[slot] = total.astype(BF16)
+            za_copy(slot, there).start()
+
+    def zb_part(e):
+        i = xback[e] * 2
+        return dot_nt(la[i], tfull[i]) + dot_nt(la[i + 1], tfull[i + 1])
+
+    def quarter(e):
+        for d in (0,) + NEAR_Z:
+            ax[d, e].wait_recv()
+
+    za_other(0)
     la_forward()
-    forward((3, 5, 4))
+    za_own(0)
+    quarter(1)
+    za_other(1)
     la_finish()
-    for d in (0,) + NEAR_Z:
-        for e in NEAR_4:
-            ax[d, e].wait_recv()
-
-    def gram_b():
-        zb = sum(dot_nt(la[i], tfull[i]) for i in range(8))
-        zall[feat, 128:256, :] = zb.astype(BF16)
-
-    za_finish = feat_scatter(
-        lambda i: dot_nn(lb[...], tfull[i]), zcs, zcr, zys, zyr, zc_s, zc_r, zy_s, zy_r, gram_b
-    )
+    zb = zb_part(0)
+    za_own(1)
+    quarter(3)
+    za_other(3)
+    zb = zb + zb_part(1)
+    za_own(3)
+    zb = zb + zb_part(3)
+    quarter(2)
+    za_other(2)
+    zb = zb + zb_part(2)
+    za_own(2)
+    zall[feat, 128:256, :] = zb.astype(BF16)
     zb_forward, zb_finish = feat_gather(
         lambda i: zall.at[i, pl.ds(128, 128), :], zby_s, zby_r, zbc_s, zbc_r
     )
-    zall[feat, 0:128, :] = za_finish().astype(BF16)
-    za_forward, za_finish2 = feat_gather(
+    for d in NEAR_4:
+        za_copy(d - 1, ys[d]).wait_recv()
+    total = zown[...] + zyr[0].astype(F32) + zyr[1].astype(F32) + zyr[2].astype(F32)
+    zall[feat, 0:128, :] = total.astype(BF16)
+    za_forward, za_finish = feat_gather(
         lambda i: zall.at[i, pl.ds(0, 128), :], zay_s, zay_r, zac_s, zac_r
     )
     zb_forward()
-    za_forward()
     zb_finish()
-    za_finish2()
 
     back[0] = rstd_a
     back[1] = rstd_b
     back[2] = factor
 
-    def gradient(n, carry):
-        cols = pl.ds(pl.multiple_of(n * 256, 256), 256)
-        g = sum(dot_nn(zall[i], pw[i * 256:(i + 1) * 256, cols]) for i in range(8))
-        ra, rb, fac = back[0, :, cols], back[1, :, cols], back[2, :, cols]
-        ha, hb = hat[0:128, cols], hat[128:256, cols]
-        qa = g[0:128] * ra
-        na = coef * qa + hb * fac
-        nb = coef * (g[128:256] * rb) + ha * fac
+    def gradient_b(n, carry):
+        cols = cols256(n)
+        g = sum(dot_nn(zall[i, 128:256, :], pw[i * 256:(i + 1) * 256, cols]) for i in range(8))
+        hb = hat[128:256, cols]
+        nb = coef * (g * back[1, :, cols]) + hat[0:128, cols] * back[2, :, cols]
+        grad[128:256, cols] = nb
+        gbx[x, 0, :, cols] = jnp.sum(nb, axis=0, keepdims=True)
+        gbx[x, 1, :, cols] = jnp.sum(nb * hb, axis=0, keepdims=True)
+        return carry
+
+    def gradient_a(n, carry):
+        cols = cols256(n)
+        g = sum(dot_nn(zall[i, 0:128, :], pw[i * 256:(i + 1) * 256, cols]) for i in range(8))
+        ha = hat[0:128, cols]
+        qa = g * back[0, :, cols]
+        na = coef * qa + hat[128:256, cols] * back[2, :, cols]
         grad[0:128, cols] = na
-        grad[128:256, cols] = nb
-        gsx[x, 0, :, cols] = jnp.sum(na, axis=0, keepdims=True)
-        gsx[x, 1, :, cols] = jnp.sum(nb, axis=0, keepdims=True)
-        gsx[x, 2, :, cols] = jnp.sum(na * ha, axis=0, keepdims=True)
-        gsx[x, 3, :, cols] = jnp.sum(nb * hb, axis=0, keepdims=True)
-        gsx[x, 4, :, cols] = jnp.sum(qa * ha, axis=0, keepdims=True)
+        gax[x, 0, :, cols] = jnp.sum(na, axis=0, keepdims=True)
+        gax[x, 1, :, cols] = jnp.sum(na * ha, axis=0, keepdims=True)
+        gax[x, 2, :, cols] = jnp.sum(qa * ha, axis=0, keepdims=True)
         return carry
 
-    lax.fori_loop(0, 4, gradient, 0)
-    gx = {d: send(gsx.at[x], gsx.at[x], gx_s.at[d - 1], gx_r.at[d - 1], xdev[d]) for d in NEAR_4}
-    for d in NEAR_4:
-        gx[d].wait_recv()
-    for i in range(5):
-        gsz[z, i] = (gsx[0, i] + gsx[1, i]) + (gsx[2, i] + gsx[3, i])
-    gz = {d: send(gsz.at[z], gsz.at[z], gz_s.at[d - 1], gz_r.at[d - 1], zdev[d]) for d in NEAR_Z}
-    for d in NEAR_Z:
-        gz[d].wait_recv()
-    sums = [sum(gsz[k, i] for k in range(NZ)) for i in range(5)]
-    means = [s * (1.0 / images) for s in sums[:4]]
-    hr[0:128, :] = (rstd_a * (grad[0:128, :] - means[0] - hat[0:128, :] * means[2])).astype(BF16)
-    hr[128:256, :] = (rstd_b * (grad[128:256, :] - means[1] - hat[128:256, :] * means[3])).astype(BF16)
-
-    share = diag + (LAMBDA / (images * images)) * jnp.sum(sums[4], axis=1, keepdims=True)
-    lo[...] = jnp.broadcast_to(share, (8, 128))
+    def over_x(buf, s_sem, r_sem):
+        return {d: send(buf.at[x], buf.at[x], s_sem.at[d - 1], r_sem.at[d - 1], xdev[d]) for d in NEAR_4}
+
+    def over_z(copies, xbuf, buf, s_sem, r_sem, rows):
+        for d in NEAR_4:
+            copies[d].wait_recv()
+        for i in range(rows):
+            buf[z, i] = (xbuf[0, i] + xbuf[1, i]) + (xbuf[2, i] + xbuf[3, i])
+        return {d: send(buf.at[z], buf.at[z], s_sem.at[d - 1], r_sem.at[d - 1], zdev[d]) for d in NEAR_Z}
+
+    lax.fori_loop(0, 4, gradient_b, 0)
+    bx = over_x(gbx, gbx_s, gbx_r)
+    za_forward()
+    bz = over_z(bx, gbx, gbz, gbz_s, gbz_r, 2)
+    za_finish()
+    lax.fori_loop(0, 4, gradient_a, 0)
+    ax = over_x(gax, gax_s, gax_r)
+    az = over_z(ax, gax, gaz, gaz_s, gaz_r, 3)
+
+    def standard(copies, buf, rows, rstd):
+        for d in NEAR_Z:
+            copies[d].wait_recv()
+        first = sum(buf[k, 0] for k in range(NZ)) * (1.0 / images)
+        second = sum(buf[k, 1] for k in range(NZ)) * (1.0 / images)
+        hr[rows, :] = (rstd * (grad[rows, :] - first - hat[rows, :] * second)).astype(BF16)
+
+    arows, brows = pl.ds(0, 128), pl.ds(128, 128)
+    standard(bz, gbz, brows, rstd_b)
+    ob_finish = feat_scatter(
+        lambda i: dot_nt(hr[brows, :], rows_of_p(i)), pcs, pcr, pys, pyr, pc_s, pc_r, py_s, py_r
+    )
+    standard(az, gaz, arows, rstd_a)
+    frob = jnp.sum(sum(gaz[k, 2] for k in range(NZ)), axis=1, keepdims=True)
+    lo[...] = jnp.broadcast_to(diag + (LAMBDA / (images * images)) * frob, (8, 128))
     lc = send(lo, lorc, lo_s.at[0], lo_r.at[0], cdev)
-    o_finish = feat_scatter(
-        lambda i: dot_nt(hr[...], rows_of_p(i)), ocs, ocr, oys, oyr, oc_s, oc_r, oy_s, oy_r
+    oa_finish = feat_scatter(
+        lambda i: dot_nt(hr[arows, :], rows_of_p(i)), ocs, ocr, oys, oyr, oc_s, oc_r, oy_s, oy_r
     )
     lc.wait_recv()
-    pair = jnp.where(core == 0, lo[...] + lorc[...], lorc[...] + lo[...])
+    pair = lo[...] + lorc[...]
     lo2[...] = pair
     lly = {d: send(lo2, lory.at[y], lo_s.at[d], lo_r.at[d], ydev[d]) for d in NEAR_4}
     lory[y] = pair
-    total = o_finish()
-    grads_ref[...] = total.astype(BF16)
+    grads_ref[128:256, :] = ob_finish().astype(BF16)
+    grads_ref[0:128, :] = oa_finish().astype(BF16)
     for d in NEAR_4:
         lly[d].wait_recv()
     loss_ref[...] = (lory[0] + lory[1]) + (lory[2] + lory[3])
+    for d in NEAR_4:
+        za_copy(d - 1, ys[d]).wait_send()
     for cp in sent:
         cp.wait_send()
 
@@ -365,10 +430,13 @@
         vmem((4, 256, 256), BF16), vmem((4, 256, 256), BF16), vmem((3, 256, 256), BF16),
         vmem((3, 256, 256), BF16), vmem((8, 128, 256), BF16), vmem((128, 256), BF16),
         vmem((4, 128, 256), BF16), vmem((4, 128, 256), BF16), vmem((3, 128, 256), BF16),
-        vmem((3, 128, 256), BF16), vmem((8, 256, 256), BF16),
-        vmem((4, 5, 1, 1024), F32), vmem((8, 5, 1, 1024), F32),
-        vmem((4, 256, 256), BF16), vmem((4, 256, 256), BF16), vmem((3, 256, 256), BF16),
-        vmem((3, 256, 256), BF16),
+        vmem((3, 128, 256), BF16), vmem((128, 256), F32), vmem((8, 256, 256), BF16),
+        vmem((4, 3, 1, 1024), F32), vmem((8, 3, 1, 1024), F32),
+        vmem((4, 2, 1, 1024), F32), vmem((8, 2, 1, 1024), F32),
+        vmem((4, 128, 256), BF16), vmem((4, 128, 256), BF16), vmem((3, 128, 256), BF16),
+        vmem((3, 128, 256), BF16),
+        vmem((4, 128, 256), BF16), vmem((4, 128, 256), BF16), vmem((3, 128, 256), BF16),
+        vmem((3, 128, 256), BF16),
         vmem((8, 128), F32), vmem((8, 128), F32), vmem((8, 128), F32), vmem((4, 8, 128), F32),
         dma((3,)),
     ]
@@ -376,7 +444,7 @@
         (3,), (3,), (3,), (7,), (7,), (7,), (8, 3),
         (3,), (7,), (4,), (3,), (3,), (4,),
         (4,), (3,), (3,), (4,), (3,), (4,),
-        (3,), (7,), (4,), (3,), (4,),
+        (3,), (7,), (3,), (7,), (4,), (3,), (4,), (3,), (4,),
     ]
     for s in sizes:
         scratch += [dma(s), dma(s)]
@@ -390,7 +458,7 @@
         out_specs=[pl.BlockSpec(memory_space=pltpu.VMEM)] * 2,
         scratch_shapes=scratch,
         compiler_params=pltpu.CompilerParams(
-            collective_id=0, has_side_effects=True, vmem_limit_bytes=63 * 1024 * 1024
+            collective_id=0, has_side_effects=True, vmem_limit_bytes=54784 * 1024
         ),
         cost_estimate=pl.CostEstimate(flops=5 * 10**9, bytes_accessed=6 * 10**6, transcendentals=0),
         name="twins",

time: 91.5 us -> 88.2 us (0.964)
  Pallas kernels: 88 us -> 86.3 us
  local copies, waits for them, and re-layouts: 2.71 us -> 1.17 us
    pallas_call x1, Pallas kernels: 88 us -> 86.3 us  [on_device(): pl.pallas_call(kernel, out_shape=(jax.ShapeDtypeStruct((8, 128), F32), ja...]
    slice x2, local copies, waits for them, and re-layouts: 2.71 us -> 1.17 us  [on_device(): return (loss[0, 0], grads[0:128], grads[128:256])]
where the time goes in v3:
time: 88.2 us; the launch traced here: 88.1 us
  Pallas kernels  86.3 us (98%)
  local copies, waits for them, and re-layouts  1.17 us (1%)
    pallas_call x1, Pallas kernels, on_device(): pl.pallas_call(kernel, out_shape=(jax.ShapeDtypeStruct((8, 128), F32), ja...  86.3 us

profile of v3, /device:TPU:1, one launch (start us, length us, event | category | flops | bytes accessed | tf_op | source)
XLA Modules:
  0.0 88.1 jit_solution(13423236125230423562)
XLA Ops:
  0.6 86.3 %twins.1 = (f32[8,128]{1,0:T(8,128)S(1)}, bf16[256,256]{1,0:T(8,128)(2,1)S(1)}) custom-call(bf16[128,2048]{1,0:T(8,128)(2,1)} %va.1, bf16[128,2048]{1,0:T(8,128)(2,1)} %vb.1, bf16[2048,1024]{1,0:T(8,128)(2,1)} %proj.1), custom_call_target="tpu_custom_call" | custom-call | flops 5000000000 | bytes 6000000 | tf_op jit(solution)/shard_map/twins/pallas_call | solution.py:451
  86.9 0.5 slice.9
  87.4 0.7 fusion

commit v4 on v3

--- a/solution.py
+++ b/solution.py
@@ -147,19 +147,21 @@
     bmean = jnp.sum(bcols, axis=0, keepdims=True) * (1.0 / 512)
     ct = (bcols - bmean).T.astype(BF16)
     mz[z, 2] = bmean
-    for d in NEAR_4:
-        xcc[d].wait_recv()
-    for h in range(2):
+    mzc, tz = {}, {}
+    for i, h in enumerate((core, 1 - core)):
+        if i == 1:
+            for d in NEAR_4:
+                xcc[d].wait_recv()
         acols = xa[h].reshape(512, 256).astype(F32)
         amean = jnp.sum(acols, axis=0, keepdims=True) * (1.0 / 512)
         mz[z, h] = amean
         tp[h] = dot_nn(ct, (acols - amean).astype(BF16)).astype(BF16)
-    mzc, tz = {}, {}
+        for d in NEAR_Z:
+            tz[d, i] = send(
+                tp.at[h, pl.ds(pl.multiple_of(zs[d] * 32, 32), 32), :], tzr.at[d - 1, h],
+                tz_s.at[d - 1, i], tz_r.at[d - 1, i], zdev[d],
+            )
     for d in NEAR_Z:
-        tz[d] = send(
-            tp.at[:, pl.ds(pl.multiple_of(zs[d] * 32, 32), 32), :], tzr.at[d - 1],
-            tz_s.at[d - 1], tz_r.at[d - 1], zdev[d],
-        )
         mzc[d] = send(mz.at[z], mz.at[z], mz_s.at[d - 1], mz_r.at[d - 1], zdev[d])
 
     for d in NEAR_Z:
@@ -180,6 +182,26 @@
     hat[128:256, :] = hat_b
     hr[128:256, :] = (hat_b * rstd_b).astype(BF16)
 
+    for d in NEAR_Z:
+        mzc[d].wait_recv()
+    am = [jnp.concatenate([mz[k, i] for k in range(NZ)], axis=0) for i in range(3)]
+    am = [m - jnp.sum(m, axis=0, keepdims=True) * (1.0 / NZ) for m in am]
+    bm = (am[2] * 512.0).T.astype(BF16)
+    zrows = pl.ds(pl.multiple_of(z * 32, 32), 32)
+    for h in range(2):
+        mcorr[h] = dot_nn(bm, am[h].astype(BF16))
+    total = tp[:, zrows, :].astype(F32) + mcorr[:, zrows, :]
+    for d in NEAR_Z:
+        tz[d, 0].wait_recv()
+        tz[d, 1].wait_recv()
+        total = total + tzr[d - 1].astype(F32)
+    tfull[pl.ds(2 * x, 2), zrows, :] = total.astype(BF16)
+    mine = tfull.at[pl.ds(2 * x, 2), zrows, :]
+    az = {d: send(mine, mine, az_s.at[d - 1], az_r.at[d - 1], zdev[d]) for d in NEAR_Z}
+    ax = {}
+    for e in NEAR_4:
+        ax[0, e] = send(mine, mine, ax_s.at[0, e - 1], ax_r.at[0, e - 1], xdev[e])
+
     def feat_scatter(chunk, cs, cr, y_send, y_recv, cs_s, cs_r, ysem_s, ysem_r):
         cc, yc = {}, {}
 
@@ -235,25 +257,6 @@
     l_finish = feat_scatter(
         lambda i: dot_nt(hr[...], rows_of_p(i)), lcs, lcr, lys, lyr, lc_s, lc_r, ly_s, ly_r
     )
-    for d in NEAR_Z:
-        mzc[d].wait_recv()
-    am = [jnp.concatenate([mz[k, i] for k in range(NZ)], axis=0) for i in range(3)]
-    am = [m - jnp.sum(m, axis=0, keepdims=True) * (1.0 / NZ) for m in am]
-    bm = (am[2] * 512.0).T.astype(BF16)
-    zrows = pl.ds(pl.multiple_of(z * 32, 32), 32)
-    for h in range(2):
-        mcorr[h] = dot_nn(bm, am[h].astype(BF16))
-    total = tp[:, zrows, :].astype(F32) + mcorr[:, zrows, :]
-    for d in NEAR_Z:
-        tz[d].wait_recv()
-        total = total + tzr[d - 1].astype(F32)
-    tfull[pl.ds(2 * x, 2), zrows, :] = total.astype(BF16)
-    mine = tfull.at[pl.ds(2 * x, 2), zrows, :]
-    az = {d: send(mine, mine, az_s.at[d - 1], az_r.at[d - 1], zdev[d]) for d in NEAR_Z}
-    ax = {}
-    for e in NEAR_4:
-        ax[0, e] = send(mine, mine, ax_s.at[0, e - 1], ax_r.at[0, e - 1], xdev[e])
-
     def piece(d, e):
         there = tfull.at[pl.ds(2 * x, 2), pl.ds(pl.multiple_of(zback[d] * 32, 32), 32), :]
         ax[d, e] = send(there, there, ax_s.at[d, e - 1], ax_r.at[d, e - 1], xdev[e])
@@ -441,7 +444,7 @@
         dma((3,)),
     ]
     sizes = [
-        (3,), (3,), (3,), (7,), (7,), (7,), (8, 3),
+        (3,), (3,), (3,), (7, 2), (7,), (7,), (8, 3),
         (3,), (7,), (4,), (3,), (3,), (4,),
         (4,), (3,), (3,), (4,), (3,), (4,),
         (3,), (7,), (3,), (7,), (4,), (3,), (4,), (3,), (4,),

time: 88.2 us -> 94.1 us (1.067)
  Pallas kernels: 86.3 us -> 92.2 us
    pallas_call x1, Pallas kernels: 86.3 us -> 92.2 us  [on_device(): pl.pallas_call(kernel, out_shape=(jax.ShapeDtypeStruct((8, 128), F32), ja...]
where the time goes in v4:
time: 94.1 us; the launch traced here: 94 us
  Pallas kernels  92.2 us (98%)
  local copies, waits for them, and re-layouts  1.17 us (1%)
    pallas_call x1, Pallas kernels, on_device(): pl.pallas_call(kernel, out_shape=(jax.ShapeDtypeStruct((8, 128), F32), ja...  92.2 us

profile of v4, /device:TPU:1, one launch (start us, length us, event | category | flops | bytes accessed | tf_op | source)
XLA Modules:
  0.0 94.0 jit_solution(10390082116777596623)
XLA Ops:
  0.6 92.2 %twins.1 = (f32[8,128]{1,0:T(8,128)S(1)}, bf16[256,256]{1,0:T(8,128)(2,1)S(1)}) custom-call(bf16[128,2048]{1,0:T(8,128)(2,1)} %va.1, bf16[128,2048]{1,0:T(8,128)(2,1)} %vb.1, bf16[2048,1024]{1,0:T(8,128)(2,1)} %proj.1), custom_call_target="tpu_custom_call" | custom-call | flops 5000000000 | bytes 6000000 | tf_op jit(solution)/shard_map/twins/pallas_call | solution.py:454
  92.8 0.5 slice.9
  93.3 0.7 fusion

commit v5 on v3

--- a/solution.py
+++ b/solution.py
@@ -147,19 +147,21 @@
     bmean = jnp.sum(bcols, axis=0, keepdims=True) * (1.0 / 512)
     ct = (bcols - bmean).T.astype(BF16)
     mz[z, 2] = bmean
-    for d in NEAR_4:
-        xcc[d].wait_recv()
-    for h in range(2):
+    mzc, tz = {}, {}
+    for i, h in enumerate((core, 1 - core)):
+        if i == 1:
+            for d in NEAR_4:
+                xcc[d].wait_recv()
         acols = xa[h].reshape(512, 256).astype(F32)
         amean = jnp.sum(acols, axis=0, keepdims=True) * (1.0 / 512)
         mz[z, h] = amean
         tp[h] = dot_nn(ct, (acols - amean).astype(BF16)).astype(BF16)
-    mzc, tz = {}, {}
+        for d in NEAR_Z:
+            tz[d, i] = send(
+                tp.at[h, pl.ds(pl.multiple_of(zs[d] * 32, 32), 32), :], tzr.at[d - 1, h],
+                tz_s.at[d - 1, i], tz_r.at[d - 1, i], zdev[d],
+            )
     for d in NEAR_Z:
-        tz[d] = send(
-            tp.at[:, pl.ds(pl.multiple_of(zs[d] * 32, 32), 32), :], tzr.at[d - 1],
-            tz_s.at[d - 1], tz_r.at[d - 1], zdev[d],
-        )
         mzc[d] = send(mz.at[z], mz.at[z], mz_s.at[d - 1], mz_r.at[d - 1], zdev[d])
 
     for d in NEAR_Z:
@@ -245,7 +247,8 @@
         mcorr[h] = dot_nn(bm, am[h].astype(BF16))
     total = tp[:, zrows, :].astype(F32) + mcorr[:, zrows, :]
     for d in NEAR_Z:
-        tz[d].wait_recv()
+        tz[d, 0].wait_recv()
+        tz[d, 1].wait_recv()
         total = total + tzr[d - 1].astype(F32)
     tfull[pl.ds(2 * x, 2), zrows, :] = total.astype(BF16)
     mine = tfull.at[pl.ds(2 * x, 2), zrows, :]
@@ -264,12 +267,12 @@
             for e in NEAR_4:
                 piece(d, e)
 
-    forward((1, 7))
+    forward((1, 7, 2, 6))
     total = l_finish()
     la[feat] = total[0:128].astype(BF16)
     lb[...] = total[128:256].astype(BF16)
     la_forward, la_finish = feat_gather(lambda i: la.at[i], lay_s, lay_r, lac_s, lac_r)
-    forward((2, 6, 3, 5, 4))
+    forward((3, 5, 4))
 
     zcc = {}
 
@@ -441,7 +444,7 @@
         dma((3,)),
     ]
     sizes = [
-        (3,), (3,), (3,), (7,), (7,), (7,), (8, 3),
+        (3,), (3,), (3,), (7, 2), (7,), (7,), (8, 3),
         (3,), (7,), (4,), (3,), (3,), (4,),
         (4,), (3,), (3,), (4,), (3,), (4,),
         (3,), (7,), (3,), (7,), (4,), (3,), (4,), (3,), (4,),

time: 88.2 us -> 88.4 us (level)
  no operation moved by 1% of the time
where the time goes in v5:
time: 88.4 us; the launch traced here: 88.3 us
  Pallas kernels  86.5 us (98%)
  local copies, waits for them, and re-layouts  1.17 us (1%)
    pallas_call x1, Pallas kernels, on_device(): pl.pallas_call(kernel, out_shape=(jax.ShapeDtypeStruct((8, 128), F32), ja...  86.5 us

profile of v5, /device:TPU:1, one launch (start us, length us, event | category | flops | bytes accessed | tf_op | source)
XLA Modules:
  0.0 88.3 jit_solution(13746946620504352281)
XLA Ops:
  0.6 86.5 %twins.1 = (f32[8,128]{1,0:T(8,128)S(1)}, bf16[256,256]{1,0:T(8,128)(2,1)S(1)}) custom-call(bf16[128,2048]{1,0:T(8,128)(2,1)} %va.1, bf16[128,2048]{1,0:T(8,128)(2,1)} %vb.1, bf16[2048,1024]{1,0:T(8,128)(2,1)} %proj.1), custom_call_target="tpu_custom_call" | custom-call | flops 5000000000 | bytes 6000000 | tf_op jit(solution)/shard_map/twins/pallas_call | solution.py:454
  87.2 0.5 slice.9
  87.7 0.7 fusion

commit v6 on v5

--- a/solution.py
+++ b/solution.py
@@ -198,10 +198,10 @@
         other(2)
         other(1)
         other(3)
+        other(0)
         own(2)
         own(1)
         own(3)
-        other(0)
         total = chunk(feat)
         cc[0].wait_recv()
         total = total + cr[0].astype(F32)

time: 88.4 us -> 87.1 us (0.985)
  Pallas kernels: 86.5 us -> 85.2 us
    pallas_call x1, Pallas kernels: 86.5 us -> 85.2 us  [on_device(): pl.pallas_call(kernel, out_shape=(jax.ShapeDtypeStruct((8, 128), F32), ja...]
where the time goes in v6:
time: 87.1 us; the launch traced here: 87 us
  Pallas kernels  85.2 us (98%)
  local copies, waits for them, and re-layouts  1.17 us (1%)
    pallas_call x1, Pallas kernels, on_device(): pl.pallas_call(kernel, out_shape=(jax.ShapeDtypeStruct((8, 128), F32), ja...  85.2 us

profile of v6, /device:TPU:1, one launch (start us, length us, event | category | flops | bytes accessed | tf_op | source)
XLA Modules:
  0.0 87.0 jit_solution(12702581797092898431)
XLA Ops:
  0.6 85.2 %twins.1 = (f32[8,128]{1,0:T(8,128)S(1)}, bf16[256,256]{1,0:T(8,128)(2,1)S(1)}) custom-call(bf16[128,2048]{1,0:T(8,128)(2,1)} %va.1, bf16[128,2048]{1,0:T(8,128)(2,1)} %vb.1, bf16[2048,1024]{1,0:T(8,128)(2,1)} %proj.1), custom_call_target="tpu_custom_call" | custom-call | flops 5000000000 | bytes 6000000 | tf_op jit(solution)/shard_map/twins/pallas_call | solution.py:454
  85.9 0.5 slice.9
  86.4 0.7 fusion

commit v7 on v6

--- a/solution.py
+++ b/solution.py
@@ -182,7 +182,7 @@
     hat[128:256, :] = hat_b
     hr[128:256, :] = (hat_b * rstd_b).astype(BF16)
 
-    def feat_scatter(chunk, cs, cr, y_send, y_recv, cs_s, cs_r, ysem_s, ysem_r):
+    def feat_scatter(chunk, cs, cr, y_send, y_recv, cs_s, cs_r, ysem_s, ysem_r, between=None):
         cc, yc = {}, {}
 
         def other(d):
@@ -199,6 +199,8 @@
         other(1)
         other(3)
         other(0)
+        if between is not None:
+            between()
         own(2)
         own(1)
         own(3)
@@ -401,14 +403,20 @@
     frob = jnp.sum(sum(gaz[k, 2] for k in range(NZ)), axis=1, keepdims=True)
     lo[...] = jnp.broadcast_to(diag + (LAMBDA / (images * images)) * frob, (8, 128))
     lc = send(lo, lorc, lo_s.at[0], lo_r.at[0], cdev)
+    lly = {}
+
+    def loss_over_y():
+        lc.wait_recv()
+        pair = lo[...] + lorc[...]
+        lo2[...] = pair
+        for d in NEAR_4:
+            lly[d] = send(lo2, lory.at[y], lo_s.at[d], lo_r.at[d], ydev[d])
+        lory[y] = pair
+
     oa_finish = feat_scatter(
-        lambda i: dot_nt(hr[arows, :], rows_of_p(i)), ocs, ocr, oys, oyr, oc_s, oc_r, oy_s, oy_r
-    )
-    lc.wait_recv()
-    pair = lo[...] + lorc[...]
-    lo2[...] = pair
-    lly = {d: send(lo2, lory.at[y], lo_s.at[d], lo_r.at[d], ydev[d]) for d in NEAR_4}
-    lory[y] = pair
+        lambda i: dot_nt(hr[arows, :], rows_of_p(i)), ocs, ocr, oys, oyr, oc_s, oc_r, oy_s, oy_r,
+        loss_over_y,
+    )
     grads_ref[128:256, :] = ob_finish().astype(BF16)
     grads_ref[0:128, :] = oa_finish().astype(BF16)
     for d in NEAR_4:

time: 87.1 us -> 87.2 us (level)
  no operation moved by 1% of the time
where the time goes in v7:
time: 87.2 us; the launch traced here: 87.1 us
  Pallas kernels  85.3 us (98%)
  local copies, waits for them, and re-layouts  1.17 us (1%)
    pallas_call x1, Pallas kernels, on_device(): pl.pallas_call(kernel, out_shape=(jax.ShapeDtypeStruct((8, 128), F32), ja...  85.3 us

profile of v7, /device:TPU:1, one launch (start us, length us, event | category | flops | bytes accessed | tf_op | source)
XLA Modules:
  0.0 87.1 jit_solution(17822497928963583270)
XLA Ops:
  0.6 85.3 %twins.1 = (f32[8,128]{1,0:T(8,128)S(1)}, bf16[256,256]{1,0:T(8,128)(2,1)S(1)}) custom-call(bf16[128,2048]{1,0:T(8,128)(2,1)} %va.1, bf16[128,2048]{1,0:T(8,128)(2,1)} %vb.1, bf16[2048,1024]{1,0:T(8,128)(2,1)} %proj.1), custom_call_target="tpu_custom_call" | custom-call | flops 5000000000 | bytes 6000000 | tf_op jit(solution)/shard_map/twins/pallas_call | solution.py:462
  85.9 0.5 slice.9
  86.4 0.7 fusion
